TPU v7x, 512 devices: a whole 4x4x16 slice. The times are simulated.
512 devices in a mesh: rows: 32 (over y, x, core), heads: 16 (over z).
Axes of the slice: x: 4, y: 4, z: 16, core: 2. Of those that a mesh axis runs over, the one named last changes fastest.
Arguments:
- pixels: float32 [8192, 768], P('rows'), may hold values from -6 to 6
- perturbation: float32 [8192, 768], P('rows'), may hold values from -0.6 to 0.6
- segment_ids: int32 [32, 256], P('rows'), may hold values from 0 to 3, never falling along the last dimension, each value on 1 to 128 neighbouring positions
- ball_radius: float32 [32, 4], P('rows'), may hold values from 0.05 to 0.4
- w_embed: bfloat16 [768, 1024], replicated, may hold values from -0.21875 to 0.21875
- gain_attn: float32 [1024], replicated, may hold values from 0.5 to 1.5
- w_qkv: bfloat16 [1024, 3, 1024], P('rows', None, 'heads'), may hold values from -0.1875 to 0.1875
- w_out: bfloat16 [1024, 1024], P('heads', 'rows'), may hold values from -0.1875 to 0.1875
- gain_mlp: float32 [1024], replicated, may hold values from 0.5 to 1.5
- w_up: bfloat16 [1024, 4096], P('rows', 'heads'), may hold values from -0.1875 to 0.1875
- w_down: bfloat16 [4096, 1024], P('heads', 'rows'), may hold values from -0.09375 to 0.09375
- out_grad: bfloat16 [8192, 1024], P('rows'), may hold values from -6 to 6
Outputs:
- block_out: bfloat16 [8192, 1024], P('rows')
- new_perturbation: float32 [8192, 768], P('rows')
Inputs may be any that keep to these rules, and one draw needn't show every extreme that they name: `segment_ids`: each pack numbers its images 0 to 3 in order along the pack; each image has 1 to 128 patches and some image of every pack has exactly 128.
All inputs are finite; a program needn't handle non-finite values.
Results may differ from a plain program's by a relative error of at most 0.019.
Values may be sent and summed in bfloat16 or wider, within the bound.
No kernel may reach another device: no remote copies, remote signals or barrier semaphores. Data moves between devices by JAX's collectives and lax.ppermute only.
A program may use at most 64 MiB of HBM per device.

v0:
```python
import math
import jax
import jax.numpy as jnp
from jax import lax
from jax.sharding import PartitionSpec as P

D = 1024
HEADS = 16
STEP_SIZE = 0.1


def layer_norm(values, gain):
    center = jnp.mean(values, -1, keepdims=True)
    shifted = values - center
    spread = jnp.mean(shifted * shifted, -1, keepdims=True)
    return shifted * lax.rsqrt(spread + 1e-05) * gain


def norm_back(values, gain, upstream):
    _, pull = jax.vjp(lambda t: layer_norm(t, gain), values)
    return pull(upstream)[0]


def gelu_back(values, upstream):
    _, pull = jax.vjp(jax.nn.gelu, values)
    return pull(upstream)[0]


def split_heads(projected):
    count, _, width = projected.shape
    size = D // HEADS
    parts = projected.reshape(count, 3, width // size, size)
    return (parts[:, 0], parts[:, 1], parts[:, 2])


def attend(projected, same):
    count, _, width = projected.shape
    query, keys, values = split_heads(projected)
    scale = 1.0 / math.sqrt(D // HEADS)
    scores = jnp.einsum("qhd,khd->hqk", query, keys, preferred_element_type=jnp.float32) * scale
    powers = jnp.where(same[None], jnp.exp(scores), 0.0)
    shares = powers / jnp.sum(powers, -1, keepdims=True)
    shares_low = shares.astype(jnp.bfloat16)
    mixed = jnp.einsum("hqk,khd->qhd", shares_low, values, preferred_element_type=jnp.float32)
    return (mixed.astype(jnp.bfloat16).reshape(count, width), shares, shares_low)


def attend_back(grad_heads, projected, shares, shares_low):
    count, _, width = projected.shape
    query, keys, values = split_heads(projected)
    size = D // HEADS
    scale = 1.0 / math.sqrt(size)
    upstream = grad_heads.reshape(count, width // size, size)
    grad_shares = jnp.einsum("qhd,khd->hqk", upstream, values, preferred_element_type=jnp.float32)
    grad_value = jnp.einsum(
        "hqk,qhd->khd", shares_low, upstream, preferred_element_type=jnp.float32
    ).astype(jnp.bfloat16)
    inner = jnp.sum(grad_shares * shares, -1, keepdims=True)
    grad_scores = (shares * (grad_shares - inner) * scale).astype(jnp.bfloat16)
    grad_query = jnp.einsum(
        "hqk,khd->qhd", grad_scores, keys, preferred_element_type=jnp.float32
    ).astype(jnp.bfloat16)
    grad_key = jnp.einsum(
        "hqk,qhd->khd", grad_scores, query, preferred_element_type=jnp.float32
    ).astype(jnp.bfloat16)
    return jnp.stack([grad_query, grad_key, grad_value], 1).reshape(count, 3, width)


def body(
    pixels,
    perturbation,
    segment_ids,
    ball_radius,
    w_embed,
    gain_attn,
    w_qkv,
    w_out,
    gain_mlp,
    w_up,
    w_down,
    out_grad,
):
    local_rows = pixels.shape[0]
    images = ball_radius.shape[1]
    patch_size = pixels.shape[1]
    w_qkv, w_out, w_up, w_down = (
        lax.all_gather(w_qkv, "rows", axis=0, tiled=True),
        lax.all_gather(w_out, "rows", axis=1, tiled=True),
        lax.all_gather(w_up, "rows", axis=0, tiled=True),
        lax.all_gather(w_down, "rows", axis=1, tiled=True),
    )
    model = w_qkv.shape[0]
    share = w_qkv.shape[2]
    labels = segment_ids[0]
    same = labels[:, None] == labels[None, :]
    inputs = (pixels + perturbation).astype(jnp.bfloat16)
    embedded = jnp.dot(inputs, w_embed, preferred_element_type=jnp.float32)
    normed_one = layer_norm(embedded, gain_attn).astype(jnp.bfloat16)
    projected = jnp.dot(
        normed_one, w_qkv.reshape(model, 3 * share), preferred_element_type=jnp.float32
    )
    projected = projected.reshape(local_rows, 3, share).astype(jnp.bfloat16)
    attended, shares, shares_low = attend(projected, same)
    attn_terms = jnp.dot(attended, w_out, preferred_element_type=jnp.float32)
    stream_mid = embedded + lax.psum(attn_terms.astype(jnp.bfloat16), "heads").astype(jnp.float32)
    normed_two = layer_norm(stream_mid, gain_mlp).astype(jnp.bfloat16)
    hidden_pre = jnp.dot(normed_two, w_up, preferred_element_type=jnp.float32)
    hidden_act = jax.nn.gelu(hidden_pre).astype(jnp.bfloat16)
    mlp_terms = jnp.dot(hidden_act, w_down, preferred_element_type=jnp.float32)
    stream_out = stream_mid + lax.psum(mlp_terms.astype(jnp.bfloat16), "heads").astype(jnp.float32)
    grad_hidden = jnp.dot(out_grad, w_down.T, preferred_element_type=jnp.float32)
    grad_pre = gelu_back(hidden_pre, grad_hidden).astype(jnp.bfloat16)
    up_terms = jnp.dot(grad_pre, w_up.T, preferred_element_type=jnp.float32)
    grad_norm_two = lax.psum(up_terms.astype(jnp.bfloat16), "heads").astype(jnp.float32)
    grad_mid = out_grad.astype(jnp.float32) + norm_back(stream_mid, gain_mlp, grad_norm_two)
    grad_mid_low = grad_mid.astype(jnp.bfloat16)
    grad_heads = jnp.dot(grad_mid_low, w_out.T, preferred_element_type=jnp.float32).astype(
        jnp.bfloat16
    )
    grad_proj = attend_back(grad_heads, projected, shares, shares_low)
    qkv_terms = jnp.einsum("tcf,dcf->td", grad_proj, w_qkv, preferred_element_type=jnp.float32)
    grad_norm_one = lax.psum(qkv_terms.astype(jnp.bfloat16), "heads").astype(jnp.float32)
    grad_embed = grad_mid + norm_back(embedded, gain_attn, grad_norm_one)
    grad_input = jnp.dot(
        grad_embed.astype(jnp.bfloat16), w_embed.T, preferred_element_type=jnp.float32
    )
    numbers = jnp.arange(images, dtype=jnp.int32)
    onehot = (labels[:, None] == numbers[None, :]).astype(jnp.float32)
    counts = jnp.sum(onehot, 0) * patch_size
    grad_sq = jnp.sum(onehot * jnp.sum(grad_input * grad_input, 1)[:, None], 0)
    scale = STEP_SIZE * lax.rsqrt(grad_sq / counts + 1e-06)
    candidate = perturbation + jnp.sum(onehot * scale[None, :], 1)[:, None] * grad_input
    cand_sq = jnp.sum(onehot * jnp.sum(candidate * candidate, 1)[:, None], 0)
    factor = jnp.minimum(1.0, ball_radius[0] * lax.rsqrt(cand_sq / counts + 1e-06))
    updated = candidate * jnp.sum(onehot * factor[None, :], 1)[:, None]
    return (stream_out.astype(jnp.bfloat16), updated)


def solution(mesh):
    in_specs = (
        P("rows", None),
        P("rows", None),
        P("rows", None),
        P("rows", None),
        P(),
        P(),
        P("rows", None, "heads"),
        P("heads", "rows"),
        P(),
        P("rows", "heads"),
        P("heads", "rows"),
        P("rows", None),
    )
    out_specs = (P("rows", None), P("rows", None))
    return jax.shard_map(body, mesh=mesh, in_specs=in_specs, out_specs=out_specs, check_vma=False)
```

profile of v0, /device:TPU:2, one launch (start us, length us, event | category | flops | bytes accessed | tf_op | source)
XLA Modules:
  0.0 501.0 jit_solution(2549400492572858672)
XLA Ops:
  7.2 29.8 %all_gather.13 = bf16[64,1024]{0,1:T(8,128)(2,1)} all-gather(bf16[64,32]{0,1:T(8,128)(2,1)} %param.19), channel_id=1, replica_groups=mesh['rows'=32,'heads'=16] {'rows'}, dimensions={1}, use_global_device_ids=true | all-gather | bytes 135168 | tf_op jit(solution)/shard_map/all_gather | solution.py:88
  37.1 23.2 %all_gather.12 = bf16[1024,3,64]{2,0,1:T(8,128)(2,1)S(1)} all-gather(bf16[32,3,64]{2,0,1:T(8,128)(2,1)} %param.18), channel_id=1, replica_groups=mesh['rows'=32,'heads'=16] {'rows'}, dimensions={0}, use_global_device_ids=true | all-gather | bytes 405504 | tf_op jit(solution)/shard_map/all_gather | solution.py:87
  60.2 0.9 copy-done.4
  61.1 1.0 copy.15
  62.1 1.8 fusion.69
  64.7 1.6 fusion.70
  66.3 2.3 convolution_convert_fusion.2
  68.7 25.9 %all_gather.14 = bf16[1024,256]{1,0:T(8,128)(2,1)} all-gather(bf16[32,256]{1,0:T(8,128)(2,1)S(1)} %copy-done.18), channel_id=1, replica_groups=mesh['rows'=32,'heads'=16] {'rows'}, dimensions={0}, use_global_device_ids=true | all-gather | bytes 540672 | tf_op jit(solution)/shard_map/all_gather | solution.py:89
  94.6 25.3 %all_gather.15 = bf16[256,1024]{0,1:T(8,128)(2,1)} all-gather(bf16[256,32]{0,1:T(8,128)(2,1)S(1)} %copy-done.19), channel_id=1, replica_groups=mesh['rows'=32,'heads'=16] {'rows'}, dimensions={1}, use_global_device_ids=true | all-gather | bytes 540672 | tf_op jit(solution)/shard_map/all_gather | solution.py:90
  119.9 85.8 %all-reduce.5.cloned.1.call-done = bf16[256,1024]{1,0:T(8,128)(2,1)} async-done(((bf16[256,1024]{1,0:T(8,128)(2,1)}), bf16[256,1024]{1,0:T(8,128)(2,1)}) %all-reduce.5.cloned.1.call-update) | async-done | bytes 524304 | tf_op jit(solution)/shard_map/psum | solution.py:105
  205.6 1.3 fusion.68
  207.2 0.7 copy-done.1
  207.9 1.1 fusion.12
  209.0 3.0 convolution_convert_fusion
  212.3 2.3 convolution_convert_fusion.1
  214.5 131.2 %all-reduce.7.cloned.1.call-done = bf16[256,1024]{1,0:T(8,128)(2,1)} async-done(((bf16[256,1024]{1,0:T(8,128)(2,1)}), bf16[256,1024]{1,0:T(8,128)(2,1)}) %all-reduce.7.cloned.1.call-update) | async-done | bytes 524304 | tf_op jit(solution)/shard_map/psum | solution.py:114
  345.7 1.8 multiply_reduce_fusion.1
  348.0 0.5 copy-done.12
  350.3 1.3 fusion
  351.6 135.9 %all-reduce.9.cloned.1.call-done = (bf16[256,1024]{1,0:T(8,128)(2,1)}, bf16[256,1024]{1,0:T(8,128)(2,1)}) async-done(((bf16[256,1024]{1,0:T(8,128)(2,1)}, bf16[256,1024]{1,0:T(8,128)(2,1)}), (bf16[256,1024]{1,0:T(8,128)(2,1)}, bf16[256,1024]{1,0:T(8,128)(2,1)})) %all-reduce.9.cloned.1.call-update) | async-done | bytes 1048592 | tf_op jit(solution)/shard_map/psum | solution.py:110
  487.4 2.7 multiply_reduce_fusion
  490.6 0.7 copy-done.7
  491.5 1.0 multiply_reduce_fusion.5
  493.3 1.1 broadcast_multiply_fusion
  (84 shorter events, 4.9 us)
Async XLA Ops:
  7.2 55.0 %copy-start = (bf16[768,1024]{1,0:T(8,128)(2,1)S(1)}, bf16[768,1024]{1,0:T(8,128)(2,1)}, u32[]{:S(2)}) copy-start(bf16[768,1024]{1,0:T(8,128)(2,1)} %param.16) | copy-start | bytes 4718596
  7.2 55.0 %copy-start.3 = (f32[256,768]{1,0:T(8,128)S(1)}, f32[256,768]{1,0:T(8,128)}, u32[]{:S(2)}) copy-start(f32[256,768]{1,0:T(8,128)} %param.13) | copy-start | bytes 2359300
  7.2 198.4 %all-reduce.5.cloned.1.call-start = ((), (), s32[]{:S(2)}) async-start(), calls=%async_computation | async-start | bytes 1048576 | tf_op jit(solution)/shard_map/psum | solution.py:105
  62.1 2.1 copy-start.11
  62.1 2.2 copy-start.17
  64.3 2.0 copy-start.24
  64.3 4.3 copy-start.22
  64.3 4.4 copy-start.18
  64.7 29.9 %copy-start.19 = (bf16[256,32]{0,1:T(8,128)(2,1)S(1)}, bf16[256,32]{0,1:T(8,128)(2,1)}, u32[]{:S(2)}) copy-start(bf16[256,32]{0,1:T(8,128)(2,1)} %param.22) | copy-start | bytes 49156
  68.6 277.1 %all-reduce.7.cloned.1.call-start = ((), (), s32[]{:S(2)}) async-start(), calls=%async_computation.1 | async-start | bytes 1048576 | tf_op jit(solution)/shard_map/psum | solution.py:114
  119.8 88.1 %copy-start.16 = (f32[1024]{0:T(1024)S(1)}, f32[1024]{0:T(1024)}, u32[]{:S(2)}) copy-start(f32[1024]{0:T(1024)} %param.20) | copy-start | bytes 12292
  205.6 2.3 copy-start.10
  212.0 275.4 %all-reduce.9.cloned.1.call-start = ((), (), s32[]{:S(2)}) async-start(), calls=%async_computation.2 | async-start | bytes 2097152 | tf_op jit(solution)/shard_map/psum | solution.py:110
  345.7 1.8 copy-start.2
  345.7 1.8 copy-start.8
  348.0 1.6 copy-start.6
  348.0 1.2 copy-start.15
  348.0 1.2 copy-start.26
  349.1 1.1 copy-start.5
  487.4 2.7 copy-start.25
  487.4 2.7 copy-start.9
  487.4 2.8 copy-start.23
  490.2 1.2 copy-start.7
  490.2 1.4 copy-start.14
  (7 other events, 6.4 us)
Sparse Core Ops, SparseCore 0:
  68.8 136.8 all-reduce.4
  212.2 133.5 all-reduce.6
  351.7 135.6 all-reduce.8
where the time goes:
time: 502 us; the launch traced here: 501 us
  waiting for transfers between devices  353 us (70%)
  blocking collectives  104 us (21%)
  matrix products  15.9 us (3%)
  between operations  14.1 us (3%)
  other arithmetic  9.03 us (2%)
    psum x1, waiting for transfers between devices, body(): lax.psum(mlp_terms.astype(jnp.bfloat16), 'heads').astype(jnp.float32)  136 us
    psum x1, waiting for transfers between devices, body(): lax.psum(up_terms.astype(jnp.bfloat16), 'heads').astype(jnp.float32)  131 us
    psum x1, waiting for transfers between devices, body(): lax.psum(attn_terms.astype(jnp.bfloat16), 'heads').astype(jnp.float32)  85.8 us
    all_gather x1, blocking collectives, body(): lax.all_gather(w_out, 'rows', axis=1, tiled=True)  29.8 us
    all_gather x1, blocking collectives, body(): lax.all_gather(w_up, 'rows', axis=0, tiled=True)  25.9 us
    all_gather x1, blocking collectives, body(): lax.all_gather(w_down, 'rows', axis=1, tiled=True)  25.3 us
    all_gather x1, blocking collectives, body(): lax.all_gather(w_qkv, 'rows', axis=0, tiled=True)  23.2 us
  transfers between devices with their start and end apart: 3, of which 3 were waited for; matrix products, arithmetic and copies ran while one was open for 0% of the time, Pallas kernels for 0%

commit v1 on v0

--- a/solution.py
+++ b/solution.py
@@ -3,10 +3,15 @@
 import jax.numpy as jnp
 from jax import lax
 from jax.sharding import PartitionSpec as P
+from jax.lax import all_gather
 
 D = 1024
 HEADS = 16
 STEP_SIZE = 0.1
+
+
+def link_the_shapes(here_x):
+    return all_gather(here_x, "heads").sum(axis=0)
 
 
 def layer_norm(values, gain):
@@ -107,7 +112,7 @@
     hidden_pre = jnp.dot(normed_two, w_up, preferred_element_type=jnp.float32)
     hidden_act = jax.nn.gelu(hidden_pre).astype(jnp.bfloat16)
     mlp_terms = jnp.dot(hidden_act, w_down, preferred_element_type=jnp.float32)
-    stream_out = stream_mid + lax.psum(mlp_terms.astype(jnp.bfloat16), "heads").astype(jnp.float32)
+    stream_out = stream_mid + link_the_shapes(mlp_terms.astype(jnp.bfloat16)).astype(jnp.float32)
     grad_hidden = jnp.dot(out_grad, w_down.T, preferred_element_type=jnp.float32)
     grad_pre = gelu_back(hidden_pre, grad_hidden).astype(jnp.bfloat16)
     up_terms = jnp.dot(grad_pre, w_up.T, preferred_element_type=jnp.float32)

time: 502 us -> 611 us (1.22)
  waiting for transfers between devices: 353 us -> 455 us
  other arithmetic: 9.03 us -> 16.4 us
    all_gather x0 -> x1, waiting for transfers between devices: none -> 103 us  [link_the_shapes(): return all_gather(here_x, 'heads').sum(axis=0)]
    reduce_sum x0 -> x1, other arithmetic: none -> 6.34 us  [link_the_shapes(): return all_gather(here_x, 'heads').sum(axis=0)]
  transfers between devices with their start and end apart: 3 -> 4, of which waited for: 3 -> 4; matrix products, arithmetic and copies ran while one was open for 0% -> 1% of each run, Pallas kernels for 0% -> 0%
where the time goes in v1:
time: 611 us; the launch traced here: 610 us
  waiting for transfers between devices  455 us (74%)
  blocking collectives  104 us (17%)
  other arithmetic  16.4 us (3%)
  matrix products  15.9 us (3%)
  between operations  14 us (2%)
    psum x1, waiting for transfers between devices, body(): lax.psum(qkv_terms.astype(jnp.bfloat16), 'heads').astype(jnp.float32)  135 us
    psum x1, waiting for transfers between devices, body(): lax.psum(up_terms.astype(jnp.bfloat16), 'heads').astype(jnp.float32)  131 us
    all_gather x1, waiting for transfers between devices, link_the_shapes(): return all_gather(here_x, 'heads').sum(axis=0)  103 us
    psum x1, waiting for transfers between devices, body(): lax.psum(attn_terms.astype(jnp.bfloat16), 'heads').astype(jnp.float32)  86.1 us
    all_gather x1, blocking collectives, body(): lax.all_gather(w_out, 'rows', axis=1, tiled=True)  30 us
    all_gather x1, blocking collectives, body(): lax.all_gather(w_up, 'rows', axis=0, tiled=True)  26.2 us
    all_gather x1, blocking collectives, body(): lax.all_gather(w_down, 'rows', axis=1, tiled=True)  24.9 us
    all_gather x1, blocking collectives, body(): lax.all_gather(w_qkv, 'rows', axis=0, tiled=True)  22.8 us
  transfers between devices with their start and end apart: 4, of which 4 were waited for; matrix products, arithmetic and copies ran while one was open for 1% of the time, Pallas kernels for 0%

profile of v1, /device:TPU:2, one launch (start us, length us, event | category | flops | bytes accessed | tf_op | source)
XLA Modules:
  0.0 610.1 jit_solution(10640472688989065488)
XLA Ops:
  7.2 30.0 %all_gather.19 = bf16[64,1024]{0,1:T(8,128)(2,1)} all-gather(bf16[64,32]{0,1:T(8,128)(2,1)} %param.19), channel_id=1, replica_groups=mesh['rows'=32,'heads'=16] {'rows'}, dimensions={1}, use_global_device_ids=true | all-gather | bytes 135168 | tf_op jit(solution)/shard_map/all_gather | solution.py:93
  37.2 22.8 %all_gather.18 = bf16[1024,3,64]{2,0,1:T(8,128)(2,1)S(1)} all-gather(bf16[32,3,64]{2,0,1:T(8,128)(2,1)} %param.18), channel_id=1, replica_groups=mesh['rows'=32,'heads'=16] {'rows'}, dimensions={0}, use_global_device_ids=true | all-gather | bytes 405504 | tf_op jit(solution)/shard_map/all_gather | solution.py:92
  60.0 0.9 copy-done.3
  60.9 1.0 copy.15
  61.9 1.8 fusion.69
  65.0 1.5 fusion.70
  66.5 2.3 convolution_convert_fusion.2
  69.0 26.2 %all_gather.20 = bf16[1024,256]{1,0:T(8,128)(2,1)} all-gather(bf16[32,256]{1,0:T(8,128)(2,1)S(1)} %copy-done.16), channel_id=1, replica_groups=mesh['rows'=32,'heads'=16] {'rows'}, dimensions={0}, use_global_device_ids=true | all-gather | bytes 540672 | tf_op jit(solution)/shard_map/all_gather | solution.py:94
  95.2 24.9 %all_gather.21 = bf16[256,1024]{0,1:T(8,128)(2,1)} all-gather(bf16[256,32]{0,1:T(8,128)(2,1)S(1)} %copy-done.17), channel_id=1, replica_groups=mesh['rows'=32,'heads'=16] {'rows'}, dimensions={1}, use_global_device_ids=true | all-gather | bytes 540672 | tf_op jit(solution)/shard_map/all_gather | solution.py:95
  120.1 86.1 %all-reduce.4.cloned.1.call-done = bf16[256,1024]{1,0:T(8,128)(2,1)} async-done(((bf16[256,1024]{1,0:T(8,128)(2,1)}), bf16[256,1024]{1,0:T(8,128)(2,1)}) %all-reduce.4.cloned.1.call-update) | async-done | bytes 524304 | tf_op jit(solution)/shard_map/psum | solution.py:110
  206.2 1.3 fusion.68
  208.6 1.1 fusion.12
  209.6 3.0 convolution_convert_fusion
  212.7 2.3 convolution_convert_fusion.1
  215.2 131.1 %all-reduce.6.cloned.1.call-done = bf16[256,1024]{1,0:T(8,128)(2,1)} async-done(((bf16[256,1024]{1,0:T(8,128)(2,1)}), bf16[256,1024]{1,0:T(8,128)(2,1)}) %all-reduce.6.cloned.1.call-update) | async-done | bytes 524304 | tf_op jit(solution)/shard_map/psum | solution.py:119
  346.3 1.7 multiply_reduce_fusion.1
  348.0 103.1 %all-gather.3.cloned.1.call-done = bf16[4096,1024]{1,0:T(8,128)(2,1)} async-done(((bf16[256,1024]{1,0:T(8,128)(2,1)}), bf16[4096,1024]{1,0:T(8,128)(2,1)}) %all-gather.3.cloned.1.call-update) | async-done | bytes 8388624 | tf_op jit(solution)/shard_map/all_gather | solution.py:14
  451.1 6.3 %reduce_sum.170 = bf16[256,1024]{1,0:T(8,128)(2,1)} reduce(bf16[16,256,1024]{2,1,0:T(8,128)(2,1)} %bitcast.88, bf16[]{:T(256)} %constant.36.clone.1), dimensions={0}, to_apply=%region_6.7 | reduce | flops 3932160 | bytes 8912898 | tf_op jit(solution)/shard_map/reduce_sum | solution.py:14
  457.5 2.8 fusion.67
  462.5 1.3 fusion
  463.8 134.9 %all-reduce.8.cloned.1.call-done = bf16[256,1024]{1,0:T(8,128)(2,1)} async-done(((bf16[256,1024]{1,0:T(8,128)(2,1)}), bf16[256,1024]{1,0:T(8,128)(2,1)}) %all-reduce.8.cloned.1.call-update) | async-done | bytes 524304 | tf_op jit(solution)/shard_map/psum | solution.py:127
  598.7 1.5 multiply_reduce_fusion
  600.6 1.0 multiply_reduce_fusion.5
  602.5 1.1 broadcast_multiply_fusion
  (82 shorter events, 6.1 us)
Async XLA Ops:
  7.2 54.7 %copy-start = (bf16[768,1024]{1,0:T(8,128)(2,1)S(1)}, bf16[768,1024]{1,0:T(8,128)(2,1)}, u32[]{:S(2)}) copy-start(bf16[768,1024]{1,0:T(8,128)(2,1)} %param.16) | copy-start | bytes 4718596
  7.2 54.7 %copy-start.2 = (f32[256,768]{1,0:T(8,128)S(1)}, f32[256,768]{1,0:T(8,128)}, u32[]{:S(2)}) copy-start(f32[256,768]{1,0:T(8,128)} %param.13) | copy-start | bytes 2359300
  7.2 199.0 %all-reduce.4.cloned.1.call-start = ((), (), s32[]{:S(2)}) async-start(), calls=%async_computation | async-start | bytes 1048576 | tf_op jit(solution)/shard_map/psum | solution.py:110
  61.9 2.7 copy-start.9
  61.9 2.7 copy-start.15
  63.8 1.3 copy-start.18
  64.6 4.3 copy-start.19
  64.6 4.4 copy-start.16
  65.0 30.2 %copy-start.17 = (bf16[256,32]{0,1:T(8,128)(2,1)S(1)}, bf16[256,32]{0,1:T(8,128)(2,1)}, u32[]{:S(2)}) copy-start(bf16[256,32]{0,1:T(8,128)(2,1)} %param.22) | copy-start | bytes 49156
  68.9 277.4 %all-reduce.6.cloned.1.call-start = ((), (), s32[]{:S(2)}) async-start(), calls=%async_computation.1 | async-start | bytes 1048576 | tf_op jit(solution)/shard_map/psum | solution.py:119
  120.1 88.4 %copy-start.14 = (f32[1024]{0:T(1024)S(1)}, f32[1024]{0:T(1024)}, u32[]{:S(2)}) copy-start(f32[1024]{0:T(1024)} %param.20) | copy-start | bytes 12292
  206.2 2.4 copy-start.8
  212.7 238.5 %all-gather.3.cloned.1.call-start = ((), (), s32[]{:S(2)}) async-start(), calls=%async_computation.3 | async-start | bytes 8912896 | tf_op jit(solution)/shard_map/all_gather | solution.py:14
  215.0 383.7 %all-reduce.8.cloned.1.call-start = ((), (), s32[]{:S(2)}) async-start(), calls=%async_computation.2 | async-start | bytes 1048576 | tf_op jit(solution)/shard_map/psum | solution.py:127
  457.5 2.8 copy-start.10
  457.5 2.8 copy-start.11
  460.3 1.6 copy-start.5
  460.3 1.1 copy-start.23
  461.4 1.1 copy-start.4
  462.5 137.6 %copy-start.22 = (f32[256]{0:T(256)S(1)}, f32[256]{0:T(256)}, u32[]{:S(2)}) copy-start(f32[256]{0:T(256)} %copy-done.21) | copy-start | bytes 3076
  462.5 137.7 %copy-start.20 = (f32[256]{0:T(256)S(1)}, f32[256]{0:T(256)}, u32[]{:S(2)}) copy-start(f32[256]{0:T(256)} %copy-done.19) | copy-start | bytes 3076
  598.7 1.5 copy-start.7
  598.7 2.0 copy-start.6
  598.7 2.0 copy-start.12
  (5 other events, 4.3 us)
Sparse Core Ops, SparseCore 0:
  69.0 137.1 all-reduce.3
  212.8 133.5 all-reduce.5
  348.4 102.6 all-gather.2
  463.9 134.6 all-reduce.7
